TPU v7x, 32 devices: a whole 2x2x4 slice. The times are simulated.
32 devices in a mesh: groups: 2 (over y), patch: 4 (over z), view: 2 (over x), head: 2 (over core).
Axes of the slice: x: 2, y: 2, z: 4, core: 2. Of those that a mesh axis runs over, the one named last changes fastest.
Arguments:
- tokens: bfloat16 [8192, 768], P(('groups', 'patch', 'view', 'head')), parts along dimension 0, may hold values from -6 to 6
- w_kv: bfloat16 [768, 1536], replicated, may hold values from -0.21875 to 0.21875
- w_rate: bfloat16 [3, 768], replicated, may hold values from -0.21875 to 0.21875
- fast_weights: bfloat16 [512, 3, 3, 256], replicated, as said below
- queries: bfloat16 [8192, 768], P(('groups', 'patch', 'view', 'head')), parts along dimension 0, may hold values from -6 to 6
- w_query: bfloat16 [768, 768], replicated, may hold values from -0.21875 to 0.21875
- out_gain: bfloat16 [768], replicated, may hold values from 0.25 to 1.75
- w_out: bfloat16 [768, 768], replicated, may hold values from -0.21875 to 0.21875
Outputs:
- decoded: bfloat16 [8192, 768], P(('groups', 'patch', 'view', 'head')), parts along dimension 0
There are 2 independent parts, one for each index of `groups`. A program takes and returns all parts, laid end to end along the dimension named above; an argument that names none is the same for every part. Nothing has to cross between parts.
Inputs may be any that keep to these rules, and one draw needn't show every extreme that they name: `fast_weights`: Real-valued entries.
All inputs are finite; a program needn't handle non-finite values.
Results may differ from a plain program's by a relative error of at most 0.035.
Values may be sent and summed in bfloat16 or wider, within the bound.
A program may use at most 64 MiB of HBM per device.

v0:
```python
import jax
import jax.numpy as jnp
from jax import lax
from jax.sharding import PartitionSpec as P

HEADS = 3
HD = 256
FF = 512
STEPS = 3


coef_a = 3.4445
coef_b = -4.775
coef_c = 2.0315
eta_rate = 3.0
eps_small = 1e-06


def unit_heads(raw):
    shaped = raw.reshape(raw.shape[0], HEADS, HD)
    return shaped / jnp.sqrt(jnp.sum(shaped * shaped, -1, keepdims=True) + eps_small)


def grad_term(keys, scaled, fast_weights):
    fp = jnp.float32
    gate_pre = jnp.einsum("thd,nhd->hnt", keys, fast_weights[:, 0], preferred_element_type=fp)
    up_pre = jnp.einsum("thd,nhd->hnt", keys, fast_weights[:, 1], preferred_element_type=fp)
    sig = jax.nn.sigmoid(gate_pre)
    act = gate_pre * sig
    hidden = (act * up_pre).astype(jnp.bfloat16)
    back = jnp.einsum("thd,nhd->hnt", scaled, fast_weights[:, 2], preferred_element_type=fp)
    d_gate = (back * up_pre * sig * (1.0 + gate_pre * (1.0 - sig))).astype(jnp.bfloat16)
    d_up = (back * act).astype(jnp.bfloat16)
    g_gate = jnp.einsum("hnt,thd->nhd", d_gate, keys, preferred_element_type=fp)
    g_up = jnp.einsum("hnt,thd->nhd", d_up, keys, preferred_element_type=fp)
    g_down = jnp.einsum("hnt,thd->nhd", hidden, scaled, preferred_element_type=fp)
    return jnp.stack([g_gate, g_up, g_down], 1)


def start_point(shard, total):
    return (shard / (jnp.sqrt(total) + eps_small)[None, :, :, None]).astype(jnp.bfloat16)


def newton(ortho, gram_total):
    fp = jnp.float32
    for step in range(STEPS):
        partial_gram = jnp.einsum("nkhi,nkhj->khij", ortho, ortho, preferred_element_type=fp)
        gram = gram_total(partial_gram).astype(jnp.bfloat16)
        square = jnp.einsum("khij,khjl->khil", gram, gram, preferred_element_type=fp)
        poly = (coef_b * gram.astype(fp) + coef_c * square).astype(jnp.bfloat16)
        mixed = jnp.einsum("nkhi,khij->nkhj", ortho, poly, preferred_element_type=fp)
        ortho = (coef_a * ortho.astype(fp) + mixed).astype(jnp.bfloat16)
    return ortho


def renorm(old_rows, ortho):
    fp = jnp.float32
    old_f = old_rows.astype(fp)
    moved = old_f + eta_rate * ortho.astype(fp)
    old_norm = jnp.sqrt(jnp.sum(old_f * old_f, -1, keepdims=True))
    new_norm = jnp.sqrt(jnp.sum(moved * moved, -1, keepdims=True)) + eps_small
    return (moved * old_norm / new_norm).astype(jnp.bfloat16)


def local(tokens, w_kv, w_rate, fast_weights, queries, w_query, out_gain, w_out):
    fp = jnp.float32
    width = tokens.shape[1]
    both = jnp.dot(tokens, w_kv, preferred_element_type=fp)
    keys = unit_heads(both[:, :width]).astype(jnp.bfloat16)
    rate = jax.nn.softplus(jnp.einsum("td,hd->th", tokens, w_rate, preferred_element_type=fp))
    scaled = (rate[:, :, None] * both[:, width:].reshape(-1, HEADS, HD)).astype(jnp.bfloat16)
    qry = unit_heads(jnp.dot(queries, w_query, preferred_element_type=fp)).astype(jnp.bfloat16)
    rows = FF // lax.axis_size("patch")
    scattered = lax.psum_scatter(
        grad_term(keys, scaled, fast_weights), "patch", scatter_dimension=0, tiled=True
    )
    shard = lax.psum(scattered, ("view", "head"))
    total = lax.psum(jnp.sum(shard * shard, axis=(0, 3)), "patch")
    begin = start_point(shard, total)
    ortho = newton(begin, lambda part: lax.psum(part, "patch"))
    own = lax.dynamic_slice_in_dim(fast_weights, lax.axis_index("patch") * rows, rows, 0)
    fresh = renorm(own, ortho)
    piece = lax.all_gather(fresh, "patch", axis=0, tiled=True)
    gate_pre = jnp.einsum("thd,nhd->hnt", qry, piece[:, 0], preferred_element_type=fp)
    up_pre = jnp.einsum("thd,nhd->hnt", qry, piece[:, 1], preferred_element_type=fp)
    q_hidden = (jax.nn.silu(gate_pre) * up_pre).astype(jnp.bfloat16)
    read = jnp.einsum("hnt,nhd->thd", q_hidden, piece[:, 2], preferred_element_type=fp)
    normed = read * lax.rsqrt(jnp.mean(read * read, -1, keepdims=True) + eps_small)
    normed = normed * out_gain.astype(fp).reshape(HEADS, HD)
    normed = normed.reshape(read.shape[0], width).astype(jnp.bfloat16)
    return jnp.dot(normed, w_out, preferred_element_type=fp).astype(jnp.bfloat16)


def solution(mesh):
    in_specs = (
        P(("groups", "patch", "view", "head"), None),
        P(),
        P(),
        P(),
        P(("groups", "patch", "view", "head"), None),
        P(),
        P(),
        P(),
    )
    out_specs = P(("groups", "patch", "view", "head"), None)
    return jax.shard_map(local, mesh=mesh, in_specs=in_specs, out_specs=out_specs, check_vma=False)
```

profile of v0, /device:TPU:7, one launch (start us, length us, event | category | flops | bytes accessed | tf_op | source)
XLA Modules:
  0.0 497.6 jit_solution(17543853494368263222)
XLA Ops:
  6.5 1.7 copy-done
  8.2 1.8 fusion.56
  12.8 2.7 fusion.33
  15.5 2.8 fusion.35
  20.7 1.9 fusion.37
  25.9 2.6 pad_maximum_fusion
  28.6 86.6 %reduce-scatter.2.cloned.1.call-done = f32[128,3,3,256]{0,3,2,1:T(8,128)} async-done(((f32[512,3,3,256]{0,3,2,1:T(8,128)}), f32[128,3,3,256]{0,3,2,1:T(8,128)}) %reduce-scatter.2.cloned.1.call-update) | async-done | bytes 1179664 | tf_op jit(solution)/shard_map/reduce_scatter | solution.py:74
  116.8 37.8 %all-reduce.5.cloned.1.call-done = f32[128,3,3,256]{0,3,2,1:T(8,128)} async-done(((f32[128,3,3,256]{0,3,2,1:T(8,128)}), f32[128,3,3,256]{0,3,2,1:T(8,128)}) %all-reduce.5.cloned.1.call-update) | async-done | bytes 1179664 | tf_op jit(solution)/shard_map/psum | solution.py:77
  156.1 9.7 %psum.36 = f32[3,3]{1,0:T(4,128)S(1)} all-reduce(f32[3,3]{1,0:T(4,128)S(1)} %multiply_reduce_fusion.1), channel_id=1, replica_groups=mesh['groups'=2,'patch'=4,'view'=2,'head'=2] {'patch'}, use_global_device_ids=true, to_apply=%region_4.5 | all-reduce | flops 9 | bytes 72 | tf_op jit(solution)/shard_map/psum | solution.py:78
  165.8 3.6 fusion.54
  169.4 81.3 %all-reduce.6 = bf16[3,3,256,256]{3,2,1,0:T(8,128)(2,1)} all-reduce(f32[3,3,256,256]{3,2,1,0:T(8,128)} %fusion.54), channel_id=1, replica_groups=mesh['groups'=2,'patch'=4,'view'=2,'head'=2] {'patch'}, use_global_device_ids=true, to_apply=%region_5.6 | all-reduce | flops 589824 | bytes 3538944 | tf_op jit(solution)/shard_map/psum | solution.py:80
  250.7 3.7 fusion.12
  254.4 1.9 fusion.57
  256.3 79.1 %all-reduce.7 = bf16[3,3,256,256]{3,2,1,0:T(8,128)(2,1)} all-reduce(f32[3,3,256,256]{3,2,1,0:T(8,128)} %fusion.57), channel_id=1, replica_groups=mesh['groups'=2,'patch'=4,'view'=2,'head'=2] {'patch'}, use_global_device_ids=true, to_apply=%region_6.7 | all-reduce | flops 589824 | bytes 3538944 | tf_op jit(solution)/shard_map/psum | solution.py:80
  335.4 3.0 fusion.13
  338.5 1.9 fusion.58
  340.3 78.1 %all-reduce.8 = bf16[3,3,256,256]{3,2,1,0:T(8,128)(2,1)} all-reduce(f32[3,3,256,256]{3,2,1,0:T(8,128)} %fusion.58), channel_id=1, replica_groups=mesh['groups'=2,'patch'=4,'view'=2,'head'=2] {'patch'}, use_global_device_ids=true, to_apply=%region_7.8 | all-reduce | flops 589824 | bytes 3538944 | tf_op jit(solution)/shard_map/psum | solution.py:80
  418.5 4.1 multiply_reduce_fusion
  422.7 2.3 divide_convert_fusion
  425.0 1.9 fusion.59
  427.0 54.0 %all-gather.2.cloned.1.call-done = bf16[512,3,3,256]{0,3,2,1:T(8,128)(2,1)} async-done(((bf16[128,3,3,256]{0,3,2,1:T(8,128)(2,1)}), bf16[512,3,3,256]{0,3,2,1:T(8,128)(2,1)}) %all-gather.2.cloned.1.call-update) | async-done | bytes 2359312 | tf_op jit(solution)/shard_map/all_gather | solution.py:83
  481.0 2.7 fusion.32
  483.7 3.6 multiply_reduce_fusion.2
  488.6 2.5 convolution_convert_fusion
  (47 shorter events, 13.0 us)
Async XLA Ops:
  6.5 1.7 copy-start
  6.5 108.6 %reduce-scatter.2.cloned.1.call-start = ((), (), s32[]{:S(2)}) async-start(), calls=%async_computation.1 | async-start | bytes 5898240 | tf_op jit(solution)/shard_map/reduce_scatter | solution.py:74
  15.5 2.8 copy-start.1
  15.5 3.9 copy-start.8
  20.7 1.9 copy-start.5
  22.6 1.4 copy-start.6
  24.1 1.1 copy-start.2
  28.5 126.1 %all-reduce.5.cloned.1.call-start = ((), (), s32[]{:S(2)}) async-start(), calls=%async_computation.2 | async-start | bytes 2359296 | tf_op jit(solution)/shard_map/psum | solution.py:77
  115.2 365.8 %all-gather.2.cloned.1.call-start = ((), (), s32[]{:S(2)}) async-start(), calls=%async_computation.3 | async-start | bytes 2949120 | tf_op jit(solution)/shard_map/all_gather | solution.py:83
  116.7 52.7 %copy-start.3 = (bf16[128,3,3,256]{0,3,2,1:T(8,128)(2,1)}, bf16[128,3,3,256]{0,3,2,1:T(8,128)(2,1)S(1)}, u32[]{:S(2)}) copy-start(bf16[128,3,3,256]{0,3,2,1:T(8,128)(2,1)S(1)} %copy.76) | copy-start | bytes 1769476
  340.3 78.1 %copy-start.4 = (bf16[128,3,3,256]{0,3,2,1:T(8,128)(2,1)S(1)}, bf16[128,3,3,256]{0,3,2,1:T(8,128)(2,1)}, u32[]{:S(2)}) copy-start(bf16[128,3,3,256]{0,3,2,1:T(8,128)(2,1)} %copy-done.3) | copy-start | bytes 1769476
  422.6 2.3 copy-start.9
  422.6 2.4 copy-start.7
Sparse Core Ops, SparseCore 0:
  28.6 86.4 reduce-scatter.1
  117.6 36.9 all-reduce.4
  425.1 55.8 all-gather.1
where the time goes:
time: 500 us; the launch traced here: 498 us
  blocking collectives  248 us (50%)
  waiting for transfers between devices  178 us (36%)
  matrix products  41.6 us (8%)
  between operations  13.3 us (3%)
  other arithmetic  8.07 us (2%)
  local copies, waits for them, and re-layouts  7.93 us (2%)
    psum x3, blocking collectives, local(): ortho = newton(begin, lambda part: lax.psum(part, 'patch'))  239 us
    reduce_scatter x1, waiting for transfers between devices, local(): lax.psum_scatter(grad_term(keys, scaled, fast_weights), 'patch', scatter_...  86.6 us
    all_gather x1, waiting for transfers between devices, local(): piece = lax.all_gather(fresh, 'patch', axis=0, tiled=True)  54 us
    psum x1, waiting for transfers between devices, local(): shard = lax.psum(scattered, ('view', 'head'))  37.8 us
    dot_general x3, matrix products, newton(): jnp.einsum('nkhi,khij->nkhj', ortho, poly, preferred_element_type=fp)  10.9 us
  transfers between devices with their start and end apart: 3, of which 3 were waited for; matrix products, arithmetic and copies ran while one was open for 1% of the time, Pallas kernels for 0%

commit v1 on v0

v1 whole, which is shorter than its diff:
```python
import functools

import jax
import jax.numpy as jnp
from jax import lax
from jax.experimental import pallas as pl
from jax.experimental.pallas import tpu as pltpu
from jax.sharding import PartitionSpec as P

HEADS = 3
HD = 256
FF = 512
STEPS = 3
KINDS = 3
ROWS = KINDS * FF
D = HEADS * HD
MESH = pl.DeviceIdType.MESH

coef_a = 3.4445
coef_b = -4.775
coef_c = 2.0315
eta_rate = 3.0
eps_small = 1e-06
fp = jnp.float32
half_type = jnp.bfloat16


def dot_nn(a, b):
    return lax.dot_general(a, b, (((1,), (0,)), ((), ())), preferred_element_type=fp)


def dot_nt(a, b):
    return lax.dot_general(a, b, (((1,), (1,)), ((), ())), preferred_element_type=fp)


def dot_tn(a, b):
    return lax.dot_general(a, b, (((0,), (0,)), ((), ())), preferred_element_type=fp)


def unit(raw):
    return (raw * lax.rsqrt(jnp.sum(raw * raw, -1, keepdims=True) + eps_small)).astype(half_type)


def head_columns(kind, head):
    start = (kind * HEADS + head) * HD
    return slice(start, start + HD)


def kernel(
    n_view, n_patch, rows,
    tokens, w_kv, w_rate, fast, queries, w_query, gain, w_out, out,
    keys, scaled, qry, grad, core_in, mid, view_in, low, patch_in, full, acc, send, recv,
):
    core, view, patch = lax.axis_index("head"), lax.axis_index("view"), lax.axis_index("patch")
    half = rows // 2
    part = half // n_view
    piece = part // n_patch

    views = [(d, d, lax.rem(view + d, n_view)) for d in range(1, n_view)]
    patches = [(d, n_view - 1 + d, lax.rem(patch + d, n_patch)) for d in range(1, n_patch)]

    barrier = pltpu.get_barrier_semaphore()
    pl.semaphore_signal(barrier, inc=1, device_id={"head": 1 - core}, device_id_type=MESH)
    for _, _, to in views:
        pl.semaphore_signal(barrier, inc=1, device_id={"view": to}, device_id_type=MESH)
    for _, _, to in patches:
        pl.semaphore_signal(barrier, inc=1, device_id={"patch": to}, device_id_type=MESH)

    started = []

    def span(start, size):
        return pl.ds(pl.multiple_of(start, 16), size)

    def launch(head, way, slot, source, target, where):
        copy = pltpu.make_async_remote_copy(
            src_ref=source, dst_ref=target,
            send_sem=send.at[head, way, slot], recv_sem=recv.at[head, way, slot],
            device_id=where, device_id_type=MESH,
        )
        copy.start()
        started.append(copy)
        return copy

    def arrive(copies):
        for copy in copies:
            copy.wait_recv()

    hops = {}

    def gradient(h):
        fast_gate = fast[:, head_columns(0, h)]
        fast_up = fast[:, head_columns(1, h)]
        fast_down = fast[:, head_columns(2, h)]
        key, val = keys[h], scaled[h]
        gate_pre = dot_nt(fast_gate, key)
        up_pre = dot_nt(fast_up, key)
        back = dot_nt(fast_down, val)
        sig = jax.nn.sigmoid(gate_pre)
        act = gate_pre * sig
        hidden = (act * up_pre).astype(half_type)
        d_gate = (back * up_pre * sig * (1.0 + gate_pre * (1.0 - sig))).astype(half_type)
        d_up = (back * act).astype(half_type)
        grad[h, 0:FF] = dot_nn(d_gate, key).astype(half_type)
        grad[h, FF:2 * FF] = dot_nn(d_up, key).astype(half_type)
        grad[h, 2 * FF:3 * FF] = dot_nn(hidden, val).astype(half_type)
        if rows > ROWS:
            grad[h, ROWS:rows] = jnp.zeros((rows - ROWS, HD), half_type)

    def scatter_core(h):
        hops[h, 0] = [
            launch(h, 0, 0, grad.at[h, span((1 - core) * half, half)], core_in.at[h], {"head": 1 - core})
        ]

    def scatter_view(h):
        arrive(hops[h, 0])
        mid[h] = (grad[h, span(core * half, half)].astype(fp) + core_in[h].astype(fp)).astype(half_type)
        hops[h, 1] = [
            launch(h, 0, slot, mid.at[h, span(to * part, part)], view_in.at[h, d - 1], {"view": to})
            for d, slot, to in views
        ]

    def scatter_patch(h):
        arrive(hops[h, 1])
        total = mid[h, span(view * part, part)].astype(fp)
        for d in range(n_view - 1):
            total = total + view_in[h, d].astype(fp)
        low[h] = total.astype(half_type)
        hops[h, 2] = [
            launch(h, 0, slot, low.at[h, span(to * piece, piece)], patch_in.at[h, d - 1], {"patch": to})
            for d, slot, to in patches
        ]

    def gather_patch(h):
        arrive(hops[h, 2])
        total = low[h, span(patch * piece, piece)].astype(fp)
        for d in range(n_patch - 1):
            total = total + patch_in[h, d].astype(fp)
        own = span(core * half + view * part + patch * piece, piece)
        full[h, own] = total.astype(half_type)
        hops[h, 3] = [
            launch(h, 1, slot, full.at[h, own], full.at[h, own], {"patch": to})
            for _, slot, to in patches
        ]

    def gather_view(h):
        arrive(hops[h, 3])
        own = span(core * half + view * part, part)
        hops[h, 4] = [
            launch(h, 1, slot, full.at[h, own], full.at[h, own], {"view": to})
            for _, slot, to in views
        ]

    def gather_core(h):
        arrive(hops[h, 4])
        own = span(core * half, half)
        hops[h, 5] = [launch(h, 1, 0, full.at[h, own], full.at[h, own], {"head": 1 - core})]

    def start_point(h):
        arrive(hops[h, 5])
        begin = []
        for kind in range(KINDS):
            summed = full[h, kind * FF:(kind + 1) * FF].astype(fp)
            norm = jnp.sqrt(jnp.sum(summed * summed, keepdims=True)) + eps_small
            begin.append((summed * (1.0 / norm)).astype(half_type))
        return begin

    def newton(ortho):
        grams = [dot_tn(x, x).astype(half_type) for x in ortho]
        polys = [
            (coef_b * g.astype(fp) + coef_c * dot_nn(g, g)).astype(half_type) for g in grams
        ]
        return [
            (coef_a * x.astype(fp) + dot_nn(x, p)).astype(half_type) for x, p in zip(ortho, polys)
        ]

    def renorm(h, ortho):
        fresh = []
        for kind in range(KINDS):
            old = fast[:, head_columns(kind, h)].astype(fp)
            moved = old + eta_rate * ortho[kind].astype(fp)
            old_norm = jnp.sqrt(jnp.sum(old * old, -1, keepdims=True))
            new_norm = jnp.sqrt(jnp.sum(moved * moved, -1, keepdims=True)) + eps_small
            fresh.append((moved * (old_norm / new_norm)).astype(half_type))
        return fresh

    def decode(h, fresh):
        gate_pre = dot_nt(qry[h], fresh[0])
        up_pre = dot_nt(qry[h], fresh[1])
        q_hidden = (gate_pre * jax.nn.sigmoid(gate_pre) * up_pre).astype(half_type)
        read = dot_nn(q_hidden, fresh[2])
        normed = read * lax.rsqrt(jnp.mean(read * read, -1, keepdims=True) + eps_small)
        normed = (normed * gain[:, h * HD:(h + 1) * HD].astype(fp)).astype(half_type)
        term = dot_nn(normed, w_out[h * HD:(h + 1) * HD, :])
        if h == 0:
            acc[...] = term
        elif h < HEADS - 1:
            acc[...] += term
        else:
            out[...] = (acc[...] + term).astype(half_type)

    rate_pre = dot_nt(tokens[...], w_rate[...])
    rate = jnp.maximum(rate_pre, 0.0) + jnp.log1p(jnp.exp(-jnp.abs(rate_pre)))
    for h in range(HEADS):
        keys[h] = unit(dot_nn(tokens[...], w_kv[:, h * HD:(h + 1) * HD]))
        values = dot_nn(tokens[...], w_kv[:, D + h * HD:D + (h + 1) * HD])
        scaled[h] = (rate[:, h:h + 1] * values).astype(half_type)

    gradient(0)
    pl.semaphore_wait(barrier, 1 + len(views) + len(patches))
    scatter_core(0)
    gradient(1)
    scatter_core(1)
    scatter_view(0)
    gradient(2)
    scatter_core(2)
    scatter_view(1)
    for h in range(HEADS):
        qry[h] = unit(dot_nn(queries[...], w_query[:, h * HD:(h + 1) * HD]))
    scatter_view(2)
    scatter_patch(0)
    scatter_patch(1)
    gather_patch(0)
    scatter_patch(2)
    gather_patch(1)
    gather_view(0)
    gather_patch(2)
    gather_view(1)
    gather_core(0)
    ortho = newton(start_point(0))
    gather_core(1)
    ortho = newton(newton(ortho))
    gather_view(2)
    decode(0, renorm(0, ortho))
    ortho = newton(start_point(1))
    gather_core(2)
    decode(1, renorm(1, newton(newton(ortho))))
    decode(2, renorm(2, newton(newton(newton(start_point(2))))))
    for copy in started:
        copy.wait_send()


def solution(mesh):
    n_view, n_patch = mesh.shape["view"], mesh.shape["patch"]
    unit_rows = 16 * 2 * n_view * n_patch
    rows = -(-ROWS // unit_rows) * unit_rows
    half = rows // 2
    part = half // n_view
    piece = part // n_patch
    hop_count = n_view + n_patch - 1

    def local(tokens, w_kv, w_rate, fast_weights, queries, w_query, out_gain, w_out):
        count, width = tokens.shape
        asked = queries.shape[0]
        return pl.pallas_call(
            functools.partial(kernel, n_view, n_patch, rows),
            out_shape=jax.ShapeDtypeStruct((asked, width), half_type),
            in_specs=[pl.BlockSpec(memory_space=pltpu.VMEM)] * 8,
            out_specs=pl.BlockSpec(memory_space=pltpu.VMEM),
            scratch_shapes=[
                pltpu.VMEM((HEADS, count, HD), half_type),
                pltpu.VMEM((HEADS, count, HD), half_type),
                pltpu.VMEM((HEADS, asked, HD), half_type),
                pltpu.VMEM((HEADS, rows, HD), half_type),
                pltpu.VMEM((HEADS, half, HD), half_type),
                pltpu.VMEM((HEADS, half, HD), half_type),
                pltpu.VMEM((HEADS, n_view - 1, part, HD), half_type),
                pltpu.VMEM((HEADS, part, HD), half_type),
                pltpu.VMEM((HEADS, n_patch - 1, piece, HD), half_type),
                pltpu.VMEM((HEADS, rows, HD), half_type),
                pltpu.VMEM((asked, width), fp),
                pltpu.SemaphoreType.DMA((HEADS, 2, hop_count)),
                pltpu.SemaphoreType.DMA((HEADS, 2, hop_count)),
            ],
            compiler_params=pltpu.CompilerParams(
                collective_id=0, has_side_effects=True, vmem_limit_bytes=48 * 1024 * 1024
            ),
        )(
            tokens, w_kv, w_rate, fast_weights.reshape(FF, KINDS * HEADS * HD),
            queries, w_query, out_gain.reshape(1, width), w_out,
        )

    shard = P(("groups", "patch", "view", "head"), None)
    in_specs = (shard, P(), P(), P(), shard, P(), P(), P())
    return jax.shard_map(local, mesh=mesh, in_specs=in_specs, out_specs=shard, check_vma=False)
```

time: 500 us -> 69.9 us (0.14)
  the two profiles are of different devices: /device:TPU:7 before, /device:TPU:0 now
where the time goes in v1:
time: 69.9 us; the launch traced here: 69.5 us
  Pallas kernels  56.7 us (81%)
  local copies, waits for them, and re-layouts  12.8 us (18%)
    pallas_call x1, Pallas kernels, local(): pl.pallas_call(functools.partial(kernel, n_view, n_patch, rows), out_shap...  56.7 us
    unnamed x16, local copies, waits for them, and re-layouts  8.31 us
    reshape x1, local copies, waits for them, and re-layouts, local(): fast_weights.reshape(FF, KINDS * HEADS * HD)  4.48 us

profile of v1, /device:TPU:0, one launch (start us, length us, event | category | flops | bytes accessed | tf_op | source)
XLA Modules:
  0.0 69.5 jit_solution(9941593844431906731)
XLA Ops:
  0.0 4.3 %copy.10 = bf16[512,3,3,256]{0,3,2,1:T(8,128)(2,1)} copy(bf16[512,3,3,256]{3,0,2,1:T(8,128)(2,1)} %param.11) | data formatting | bytes 4718592 | tf_op args[3]
  4.3 0.0 copy-start.6
  4.3 0.0 copy-start
  4.3 0.0 copy-start.1
  4.3 0.0 copy-start.5
  4.3 4.5 %copy.11.fast = bf16[512,2304]{1,0:T(8,128)(2,1)} copy(bf16[512,2304]{0,1:T(8,128)(2,1)} %bitcast.1) | data formatting | bytes 4718592 | tf_op jit(solution)/shard_map/reshape | solution.py:278
  8.8 0.0 copy-done.6
  8.8 0.0 copy-done
  8.8 0.0 copy-done.1
  8.8 0.0 copy-done.5
  8.8 0.0 copy-start.2
  8.8 1.3 %copy-done.2 = bf16[768,768]{1,0:T(8,128)(2,1)S(1)} copy-done((bf16[768,768]{1,0:T(8,128)(2,1)S(1)}, bf16[768,768]{1,0:T(8,128)(2,1)}, u32[]{:S(2)}) %copy-start.2) | copy-done | bytes 1179672
  10.1 0.0 copy-start.3
  10.1 1.0 %copy-done.3 = bf16[256,768]{1,0:T(8,128)(2,1)S(1)} copy-done((bf16[256,768]{1,0:T(8,128)(2,1)S(1)}, bf16[256,768]{1,0:T(8,128)(2,1)}, u32[]{:S(2)}) %copy-start.3) | copy-done | bytes 393240
  11.1 0.0 copy-start.4
  11.1 1.0 %copy-done.4 = bf16[256,768]{1,0:T(8,128)(2,1)S(1)} copy-done((bf16[256,768]{1,0:T(8,128)(2,1)S(1)}, bf16[256,768]{1,0:T(8,128)(2,1)}, u32[]{:S(2)}) %copy-start.4) | copy-done | bytes 393240
  12.1 56.7 %shard_map.82 = bf16[256,768]{1,0:T(8,128)(2,1)S(1)} custom-call(bf16[256,768]{1,0:T(8,128)(2,1)S(1)} %copy-done.3, bf16[768,1536]{1,0:T(8,128)(2,1)S(1)} %copy-done, bf16[3,768]{1,0:T(4,128)(2,1)S(1)} %copy-done.5, bf16[512,2304]{1,0:T(8,128)(2,1)} %copy.11.fast, bf16[256,768]{1,0:T(8,128)(2,1)S(1)} %copy-done.4, bf16[768,768]{1,0:T(8,128)(2,1)S(1)} %copy-done.1, ...), custom_call_target="tpu_custom_call" | custom-call | tf_op jit(solution)/shard_map/pallas_call | solution.py:254
  68.8 0.7 %copy.13 = bf16[256,768]{1,0:T(8,128)(2,1)} copy(bf16[256,768]{1,0:T(8,128)(2,1)S(1)} %shard_map.82) | data formatting | bytes 786432
  (1 shorter events, 0.0 us)
Async XLA Ops:
  4.3 4.5 %copy-start.6 = (bf16[768]{0:T(1024)(128)(2,1)S(1)}, bf16[768]{0:T(1024)(128)(2,1)}, u32[]{:S(2)}) copy-start(bf16[768]{0:T(1024)(128)(2,1)} %param.14) | copy-start | bytes 4612
  4.3 4.5 %copy-start = (bf16[768,1536]{1,0:T(8,128)(2,1)S(1)}, bf16[768,1536]{1,0:T(8,128)(2,1)}, u32[]{:S(2)}) copy-start(bf16[768,1536]{1,0:T(8,128)(2,1)} %w_kv.1) | copy-start | bytes 7077892
  4.3 4.5 %copy-start.1 = (bf16[768,768]{1,0:T(8,128)(2,1)S(1)}, bf16[768,768]{1,0:T(8,128)(2,1)}, u32[]{:S(2)}) copy-start(bf16[768,768]{1,0:T(8,128)(2,1)} %w_query.1) | copy-start | bytes 3538948
  4.3 4.5 %copy-start.5 = (bf16[3,768]{1,0:T(4,128)(2,1)S(1)}, bf16[3,768]{1,0:T(4,128)(2,1)}, u32[]{:S(2)}) copy-start(bf16[3,768]{1,0:T(4,128)(2,1)} %w_rate.1) | copy-start | bytes 13828
  8.8 1.3 %copy-start.2 = (bf16[768,768]{1,0:T(8,128)(2,1)S(1)}, bf16[768,768]{1,0:T(8,128)(2,1)}, u32[]{:S(2)}) copy-start(bf16[768,768]{1,0:T(8,128)(2,1)} %w_out.1) | copy-start | bytes 3538948
  10.1 1.0 %copy-start.3 = (bf16[256,768]{1,0:T(8,128)(2,1)S(1)}, bf16[256,768]{1,0:T(8,128)(2,1)}, u32[]{:S(2)}) copy-start(bf16[256,768]{1,0:T(8,128)(2,1)} %tokens.1) | copy-start | bytes 1179652
  11.1 1.0 %copy-start.4 = (bf16[256,768]{1,0:T(8,128)(2,1)S(1)}, bf16[256,768]{1,0:T(8,128)(2,1)}, u32[]{:S(2)}) copy-start(bf16[256,768]{1,0:T(8,128)(2,1)} %queries.1) | copy-start | bytes 1179652

commit v2 on v0

v2 whole, which is shorter than its diff:
```python
import functools

import jax
import jax.numpy as jnp
from jax import lax
from jax.experimental import pallas as pl
from jax.experimental.pallas import tpu as pltpu
from jax.sharding import PartitionSpec as P

HEADS = 3
HD = 256
FF = 512
STEPS = 3
KINDS = 3
MATS = KINDS * HEADS
D = HEADS * HD
MESH = pl.DeviceIdType.MESH

coef_a = 3.4445
coef_b = -4.775
coef_c = 2.0315
eta_rate = 3.0
eps_small = 1e-06
fp = jnp.float32
half_type = jnp.bfloat16


def dot_nn(a, b):
    return lax.dot_general(a, b, (((1,), (0,)), ((), ())), preferred_element_type=fp)


def dot_nt(a, b):
    return lax.dot_general(a, b, (((1,), (1,)), ((), ())), preferred_element_type=fp)


def dot_tn(a, b):
    return lax.dot_general(a, b, (((0,), (0,)), ((), ())), preferred_element_type=fp)


def unit(raw):
    return (raw * lax.rsqrt(jnp.sum(raw * raw, -1, keepdims=True) + eps_small)).astype(half_type)


def kernel(
    n_view, n_patch,
    tokens_hbm, w_kv_hbm, w_rate, fast_hbm, queries_hbm, w_query_hbm, gain, w_out_hbm, out,
    tokens, w_kv, fast, queries, w_query, w_out,
    keys, scaled, qry, grad, core_in, mid, view_in, low, patch_in, full, fresh, acc,
    load, send, recv,
):
    core, view, patch = lax.axis_index("head"), lax.axis_index("view"), lax.axis_index("patch")
    piece = FF // n_patch
    patches = [(d, lax.rem(patch + d, n_patch)) for d in range(1, n_patch)]
    loads = []

    def fetch(source, target):
        copy = pltpu.make_async_copy(source, target, load.at[len(loads)])
        copy.start()
        loads.append(copy)
        return copy

    get_tokens = fetch(tokens_hbm, tokens)
    get_kv = fetch(w_kv_hbm, w_kv)
    get_fast = [fetch(fast_hbm.at[:, h], fast.at[:, h]) for h in range(HEADS)]
    get_query = [fetch(queries_hbm, queries), fetch(w_query_hbm, w_query)]
    get_out = fetch(w_out_hbm, w_out)

    barrier = pltpu.get_barrier_semaphore()
    pl.semaphore_signal(barrier, inc=1, device_id={"head": 1 - core}, device_id_type=MESH)
    for d in range(1, n_view):
        pl.semaphore_signal(
            barrier, inc=1, device_id={"view": lax.rem(view + d, n_view)}, device_id_type=MESH
        )
    for _, to in patches:
        pl.semaphore_signal(barrier, inc=1, device_id={"patch": to}, device_id_type=MESH)

    core_sum, core_share = 0, 1
    view_sum = 2
    view_share = view_sum + n_view - 1
    patch_sum = view_share + n_view - 1
    patch_share = patch_sum + n_patch - 1

    def owner(m):
        slot = m % (2 * n_view)
        return slot % n_view, slot // n_view

    def remote(m, slot, source, target, where):
        return pltpu.make_async_remote_copy(
            src_ref=source, dst_ref=target, send_sem=send.at[m, slot], recv_sem=recv.at[m, slot],
            device_id=where, device_id_type=MESH,
        )

    def sum_over_core(m):
        return remote(m, core_sum, grad.at[m], core_in.at[m], {"head": 1 - core})

    def sum_over_view(m, d):
        return remote(m, view_sum + d - 1, mid.at[m], view_in.at[m, d - 1], {"view": owner(m)[0]})

    def sum_over_patch(m, d, to):
        start = pl.multiple_of(to * piece, 16)
        return remote(
            m, patch_sum + d - 1, low.at[m, pl.ds(start, piece)], patch_in.at[m, d - 1], {"patch": to}
        )

    def share_over_patch(m, d, to):
        own = full.at[m, pl.ds(pl.multiple_of(patch * piece, 16), piece)]
        return remote(m, patch_share + d - 1, own, own, {"patch": to})

    def share_over_view(m, d):
        to = (owner(m)[0] + d) % n_view
        return remote(m, view_share + d - 1, fresh.at[m], fresh.at[m], {"view": to})

    def share_over_core(m):
        return remote(m, core_share, fresh.at[m], fresh.at[m], {"head": 1 - core})

    def at_owner(m):
        return jnp.logical_and(core == owner(m)[1], view == owner(m)[0])

    def at_view(m, v):
        return jnp.logical_and(core == owner(m)[1], view == v % n_view)

    def gradient(h):
        get_fast[h].wait()
        key, val = keys[h], scaled[h]
        gate_pre = dot_nt(fast[0, h], key)
        up_pre = dot_nt(fast[1, h], key)
        back = dot_nt(fast[2, h], val)
        sig = jax.nn.sigmoid(gate_pre)
        act = gate_pre * sig
        hidden = (act * up_pre).astype(half_type)
        d_gate = (back * up_pre * sig * (1.0 + gate_pre * (1.0 - sig))).astype(half_type)
        d_up = (back * act).astype(half_type)
        grad[h * KINDS] = dot_nn(d_gate, key).astype(half_type)
        grad[h * KINDS + 1] = dot_nn(d_up, key).astype(half_type)
        grad[h * KINDS + 2] = dot_nn(hidden, val).astype(half_type)

    def stage_core(m):
        @pl.when(core != owner(m)[1])
        def _():
            sum_over_core(m).start()

    def stage_view(m):
        @pl.when(core == owner(m)[1])
        def _():
            sum_over_core(m).wait_recv()
            mid[m] = (grad[m].astype(fp) + core_in[m].astype(fp)).astype(half_type)

        for d in range(1, n_view):
            @pl.when(at_view(m, owner(m)[0] - d))
            def _():
                sum_over_view(m, d).start()

    def stage_patch(m):
        @pl.when(at_owner(m))
        def _():
            total = mid[m].astype(fp)
            for d in range(1, n_view):
                sum_over_view(m, d).wait_recv()
                total = total + view_in[m, d - 1].astype(fp)
            low[m] = total.astype(half_type)
            for d, to in patches:
                sum_over_patch(m, d, to).start()

    def stage_gather(m):
        @pl.when(at_owner(m))
        def _():
            own = pl.ds(pl.multiple_of(patch * piece, 16), piece)
            total = low[m, own].astype(fp)
            for d, to in patches:
                sum_over_patch(m, d, to).wait_recv()
                total = total + patch_in[m, d - 1].astype(fp)
            full[m, own] = total.astype(half_type)
            for d, to in patches:
                share_over_patch(m, d, to).start()

    def newton(x):
        gram = dot_tn(x, x).astype(half_type)
        poly = (coef_b * gram.astype(fp) + coef_c * dot_nn(gram, gram)).astype(half_type)
        return (coef_a * x.astype(fp) + dot_nn(x, poly)).astype(half_type)

    def stage_update(m):
        @pl.when(at_owner(m))
        def _():
            for d, to in patches:
                share_over_patch(m, d, to).wait_recv()
            summed = full[m].astype(fp)
            norm = jnp.sqrt(jnp.sum(summed * summed, keepdims=True)) + eps_small
            ortho = (summed * (1.0 / norm)).astype(half_type)
            for _ in range(STEPS):
                ortho = newton(ortho)
            old = fast[m % KINDS, m // KINDS].astype(fp)
            moved = old + eta_rate * ortho.astype(fp)
            old_norm = jnp.sqrt(jnp.sum(old * old, -1, keepdims=True))
            new_norm = jnp.sqrt(jnp.sum(moved * moved, -1, keepdims=True)) + eps_small
            fresh[m] = (moved * (old_norm / new_norm)).astype(half_type)
            for d in range(1, n_view):
                share_over_view(m, d).start()
            share_over_core(m).start()

    def stage_spread(m):
        for d in range(1, n_view):
            @pl.when(at_view(m, owner(m)[0] + d))
            def _():
                share_over_view(m, d).wait_recv()
                share_over_core(m).start()

    def decode(h):
        for m in range(h * KINDS, (h + 1) * KINDS):
            @pl.when(core != owner(m)[1])
            def _():
                share_over_core(m).wait_recv()
        gate_pre = dot_nt(qry[h], fresh[h * KINDS])
        up_pre = dot_nt(qry[h], fresh[h * KINDS + 1])
        q_hidden = (gate_pre * jax.nn.sigmoid(gate_pre) * up_pre).astype(half_type)
        read = dot_nn(q_hidden, fresh[h * KINDS + 2])
        normed = read * lax.rsqrt(jnp.mean(read * read, -1, keepdims=True) + eps_small)
        normed = (normed * gain[:, h * HD:(h + 1) * HD].astype(fp)).astype(half_type)
        term = dot_nn(normed, w_out[h * HD:(h + 1) * HD, :])
        if h == 0:
            acc[...] = term
        elif h < HEADS - 1:
            acc[...] += term
        else:
            out[...] = (acc[...] + term).astype(half_type)

    def finish(m):
        @pl.when(core != owner(m)[1])
        def _():
            sum_over_core(m).wait_send()

        for d in range(1, n_view):
            @pl.when(at_view(m, owner(m)[0] - d))
            def _():
                sum_over_view(m, d).wait_send()

        @pl.when(at_owner(m))
        def _():
            for d, to in patches:
                sum_over_patch(m, d, to).wait_send()
                share_over_patch(m, d, to).wait_send()
            for d in range(1, n_view):
                share_over_view(m, d).wait_send()

        @pl.when(core == owner(m)[1])
        def _():
            share_over_core(m).wait_send()

    get_tokens.wait()
    rate_pre = dot_nt(tokens[...], w_rate[...])
    rate = jnp.maximum(rate_pre, 0.0) + jnp.log1p(jnp.exp(-jnp.abs(rate_pre)))
    get_kv.wait()
    first, second, last = [range(h * KINDS, (h + 1) * KINDS) for h in range(HEADS)]

    def project(h):
        keys[h] = unit(dot_nn(tokens[...], w_kv[:, h * HD:(h + 1) * HD]))
        values = dot_nn(tokens[...], w_kv[:, D + h * HD:D + (h + 1) * HD])
        scaled[h] = (rate[:, h:h + 1] * values).astype(half_type)

    def run(stage, chosen):
        for m in chosen:
            stage(m)

    project(0)
    gradient(0)
    pl.semaphore_wait(barrier, n_view + n_patch - 1)
    run(stage_core, first)
    project(1)
    run(stage_view, first)
    gradient(1)
    run(stage_core, second)
    project(2)
    run(stage_view, second)
    gradient(2)
    run(stage_core, last)
    for copy in get_query:
        copy.wait()
    for h in range(HEADS):
        qry[h] = unit(dot_nn(queries[...], w_query[:, h * HD:(h + 1) * HD]))
        if h == 0:
            run(stage_view, last)
    get_out.wait()
    early, late, rest = range(0, 4), range(4, 8), range(8, MATS)
    run(stage_patch, early)
    run(stage_gather, early)
    run(stage_patch, late)
    run(stage_update, early)
    run(stage_gather, late)
    run(stage_patch, rest)
    run(stage_spread, early)
    run(stage_update, late)
    run(stage_gather, rest)
    decode(0)
    run(stage_spread, late)
    run(stage_update, rest)
    decode(1)
    run(stage_spread, rest)
    decode(2)
    run(finish, range(MATS))


def solution(mesh):
    n_view, n_patch = mesh.shape["view"], mesh.shape["patch"]
    piece = FF // n_patch
    slots = 2 * (n_view + n_patch - 1)

    def local(tokens, w_kv, w_rate, fast_weights, queries, w_query, out_gain, w_out):
        count, width = tokens.shape
        asked = queries.shape[0]
        vmem = pl.BlockSpec(memory_space=pltpu.VMEM)
        hbm = pl.BlockSpec(memory_space=pl.ANY)
        whole = pltpu.VMEM((MATS, FF, HD), half_type)
        return pl.pallas_call(
            functools.partial(kernel, n_view, n_patch),
            out_shape=jax.ShapeDtypeStruct((asked, width), half_type),
            in_specs=[hbm, hbm, vmem, hbm, hbm, hbm, vmem, hbm],
            out_specs=vmem,
            scratch_shapes=[
                pltpu.VMEM((count, width), half_type),
                pltpu.VMEM((width, 2 * width), half_type),
                pltpu.VMEM((KINDS, HEADS, FF, HD), half_type),
                pltpu.VMEM((asked, width), half_type),
                pltpu.VMEM((width, width), half_type),
                pltpu.VMEM((width, width), half_type),
                pltpu.VMEM((HEADS, count, HD), half_type),
                pltpu.VMEM((HEADS, count, HD), half_type),
                pltpu.VMEM((HEADS, asked, HD), half_type),
                whole,
                whole,
                whole,
                pltpu.VMEM((MATS, n_view - 1, FF, HD), half_type),
                whole,
                pltpu.VMEM((MATS, n_patch - 1, piece, HD), half_type),
                whole,
                whole,
                pltpu.VMEM((asked, width), fp),
                pltpu.SemaphoreType.DMA((5 + HEADS,)),
                pltpu.SemaphoreType.DMA((MATS, slots)),
                pltpu.SemaphoreType.DMA((MATS, slots)),
            ],
            compiler_params=pltpu.CompilerParams(
                collective_id=0, has_side_effects=True, vmem_limit_bytes=56 * 1024 * 1024
            ),
        )(
            tokens, w_kv, w_rate, jnp.transpose(fast_weights, (1, 2, 0, 3)),
            queries, w_query, out_gain.reshape(1, width), w_out,
        )

    shard = P(("groups", "patch", "view", "head"), None)
    in_specs = (shard, P(), P(), P(), shard, P(), P(), P())
    return jax.shard_map(local, mesh=mesh, in_specs=in_specs, out_specs=shard, check_vma=False)
```

time: 500 us -> 64.3 us (0.13)
  blocking collectives: 248 us -> 0 us
  waiting for transfers between devices: 178 us -> 0 us
  Pallas kernels: 0 us -> 61 us
  matrix products: 41.6 us -> 0 us
  between operations: 13.3 us -> 0.01 us
  other arithmetic: 8.07 us -> 0 us
    psum x4 -> x0, blocking collectives: 248 us -> none  [the longest x3 239 us: local(): ortho = newton(begin, lambda part: lax.psum(part, 'patch'))]
    reduce_scatter x1 -> x0, waiting for transfers between devices: 86.6 us -> none  [local(): lax.psum_scatter(grad_term(keys, scaled, fast_weights), 'patch', scatter_...]
    pallas_call x0 -> x1, Pallas kernels: none -> 61 us  [local(): pl.pallas_call(functools.partial(kernel, n_view, n_patch), out_shape=jax....]
    all_gather x1 -> x0, waiting for transfers between devices: 54 us -> none  [local(): piece = lax.all_gather(fresh, 'patch', axis=0, tiled=True)]
    dot_general x18 -> x0, matrix products: 41.6 us -> none  [the longest x3 10.9 us: newton(): jnp.einsum('nkhi,khij->nkhj', ortho, poly, preferred_element_type=fp)]
    psum x1 -> x0, waiting for transfers between devices: 37.8 us -> none  [local(): shard = lax.psum(scattered, ('view', 'head'))]
  transfers between devices with their start and end apart: 3 -> 0, of which waited for: 3 -> 0; matrix products, arithmetic and copies ran while one was open for 1% -> 0% of each run, Pallas kernels for 0% -> 0%
where the time goes in v2:
time: 64.3 us; the launch traced here: 64.1 us
  Pallas kernels  61 us (95%)
  local copies, waits for them, and re-layouts  3.03 us (5%)
    pallas_call x1, Pallas kernels, local(): pl.pallas_call(functools.partial(kernel, n_view, n_patch), out_shape=jax....  61 us
    unnamed x1, local copies, waits for them, and re-layouts  1.77 us

profile of v2, /device:TPU:7, one launch (start us, length us, event | category | flops | bytes accessed | tf_op | source)
XLA Modules:
  0.0 64.1 jit_solution(16570123538687108750)
XLA Ops:
  0.0 1.3 %reshape.3.gain = bf16[1,768]{1,0:T(2,128)(2,1)} reshape(bf16[768]{0:T(1024)(128)(2,1)} %param.14) | data formatting | bytes 3072 | tf_op jit(solution)/shard_map/reshape | solution.py:345
  1.3 61.0 %shard_map.82 = bf16[256,768]{1,0:T(8,128)(2,1)} custom-call(bf16[256,768]{1,0:T(8,128)(2,1)} %tokens_hbm.1, bf16[768,1536]{1,0:T(8,128)(2,1)} %w_kv_hbm.1, bf16[3,768]{1,0:T(4,128)(2,1)} %w_rate.1, bf16[3,3,512,256]{3,2,1,0:T(8,128)(2,1)} %bitcast.1, bf16[256,768]{1,0:T(8,128)(2,1)} %queries_hbm.1, bf16[768,768]{1,0:T(8,128)(2,1)} %w_query_hbm.1, ...), custom_call_target="tpu_custom_call" | custom-call | tf_op jit(solution)/shard_map/pallas_call | solution.py:312
  62.3 1.8 %copy.10 = bf16[256,768]{1,0:T(8,128)(2,1)} copy(bf16[256,768]{1,0:T(8,128)(2,1)} %shard_map.82) | data formatting | bytes 786432

commit v3 on v2

--- a/solution.py
+++ b/solution.py
@@ -60,8 +60,13 @@
         return copy
 
     get_tokens = fetch(tokens_hbm, tokens)
-    get_kv = fetch(w_kv_hbm, w_kv)
-    get_fast = [fetch(fast_hbm.at[:, h], fast.at[:, h]) for h in range(HEADS)]
+    get_kv, get_fast = [], []
+    for h in range(HEADS):
+        get_kv.append([
+            fetch(w_kv_hbm.at[:, start:start + HD], w_kv.at[:, start:start + HD])
+            for start in (h * HD, D + h * HD)
+        ])
+        get_fast.append(fetch(fast_hbm.at[:, h], fast.at[:, h]))
     get_query = [fetch(queries_hbm, queries), fetch(w_query_hbm, w_query)]
     get_out = fetch(w_out_hbm, w_out)
 
@@ -214,7 +219,7 @@
         q_hidden = (gate_pre * jax.nn.sigmoid(gate_pre) * up_pre).astype(half_type)
         read = dot_nn(q_hidden, fresh[h * KINDS + 2])
         normed = read * lax.rsqrt(jnp.mean(read * read, -1, keepdims=True) + eps_small)
-        normed = (normed * gain[:, h * HD:(h + 1) * HD].astype(fp)).astype(half_type)
+        normed = (normed * gain[h * HD:(h + 1) * HD].astype(fp)[None, :]).astype(half_type)
         term = dot_nn(normed, w_out[h * HD:(h + 1) * HD, :])
         if h == 0:
             acc[...] = term
@@ -248,10 +253,11 @@
     get_tokens.wait()
     rate_pre = dot_nt(tokens[...], w_rate[...])
     rate = jnp.maximum(rate_pre, 0.0) + jnp.log1p(jnp.exp(-jnp.abs(rate_pre)))
-    get_kv.wait()
     first, second, last = [range(h * KINDS, (h + 1) * KINDS) for h in range(HEADS)]
 
     def project(h):
+        for copy in get_kv[h]:
+            copy.wait()
         keys[h] = unit(dot_nn(tokens[...], w_kv[:, h * HD:(h + 1) * HD]))
         values = dot_nn(tokens[...], w_kv[:, D + h * HD:D + (h + 1) * HD])
         scaled[h] = (rate[:, h:h + 1] * values).astype(half_type)
@@ -283,15 +289,15 @@
     run(stage_patch, early)
     run(stage_gather, early)
     run(stage_patch, late)
-    run(stage_update, early)
     run(stage_gather, late)
     run(stage_patch, rest)
+    run(stage_update, early)
+    run(stage_gather, rest)
+    run(stage_update, late)
     run(stage_spread, early)
-    run(stage_update, late)
-    run(stage_gather, rest)
+    run(stage_update, rest)
+    run(stage_spread, late)
     decode(0)
-    run(stage_spread, late)
-    run(stage_update, rest)
     decode(1)
     run(stage_spread, rest)
     decode(2)
@@ -333,7 +339,7 @@
                 whole,
                 whole,
                 pltpu.VMEM((asked, width), fp),
-                pltpu.SemaphoreType.DMA((5 + HEADS,)),
+                pltpu.SemaphoreType.DMA((4 + 3 * HEADS,)),
                 pltpu.SemaphoreType.DMA((MATS, slots)),
                 pltpu.SemaphoreType.DMA((MATS, slots)),
             ],
@@ -342,7 +348,7 @@
             ),
         )(
             tokens, w_kv, w_rate, jnp.transpose(fast_weights, (1, 2, 0, 3)),
-            queries, w_query, out_gain.reshape(1, width), w_out,
+            queries, w_query, out_gain, w_out,
         )
 
     shard = P(("groups", "patch", "view", "head"), None)

time: 64.3 us -> 61.3 us (0.953)
  Pallas kernels: 61 us -> 59.3 us
  local copies, waits for them, and re-layouts: 3.03 us -> 1.77 us
    pallas_call x1, Pallas kernels: 61 us -> 59.3 us  [local(): pl.pallas_call(functools.partial(kernel, n_view, n_patch), out_shape=jax....]
    reshape x1 -> x0, local copies, waits for them, and re-layouts: 1.26 us -> none  [local(): out_gain.reshape(1, width)]
where the time goes in v3:
time: 61.3 us; the launch traced here: 61.1 us
  Pallas kernels  59.3 us (97%)
  local copies, waits for them, and re-layouts  1.77 us (3%)
    pallas_call x1, Pallas kernels, local(): pl.pallas_call(functools.partial(kernel, n_view, n_patch), out_shape=jax....  59.3 us
    unnamed x1, local copies, waits for them, and re-layouts  1.77 us

profile of v3, /device:TPU:7, one launch (start us, length us, event | category | flops | bytes accessed | tf_op | source)
XLA Modules:
  0.0 61.1 jit_solution(5458035751623719098)
XLA Ops:
  0.0 59.3 %shard_map.82 = bf16[256,768]{1,0:T(8,128)(2,1)} custom-call(bf16[256,768]{1,0:T(8,128)(2,1)} %tokens_hbm.1, bf16[768,1536]{1,0:T(8,128)(2,1)} %w_kv_hbm.1, bf16[3,768]{1,0:T(4,128)(2,1)} %w_rate.1, bf16[3,3,512,256]{3,2,1,0:T(8,128)(2,1)} %bitcast.1, bf16[256,768]{1,0:T(8,128)(2,1)} %queries_hbm.1, bf16[768,768]{1,0:T(8,128)(2,1)} %w_query_hbm.1, ...), custom_call_target="tpu_custom_call" | custom-call | tf_op jit(solution)/shard_map/pallas_call | solution.py:318
  59.3 1.8 %copy.10 = bf16[256,768]{1,0:T(8,128)(2,1)} copy(bf16[256,768]{1,0:T(8,128)(2,1)} %shard_map.82) | data formatting | bytes 786432

commit v4 on v3

--- a/solution.py
+++ b/solution.py
@@ -49,8 +49,15 @@
     load, send, recv,
 ):
     core, view, patch = lax.axis_index("head"), lax.axis_index("view"), lax.axis_index("patch")
-    piece = FF // n_patch
-    patches = [(d, lax.rem(patch + d, n_patch)) for d in range(1, n_patch)]
+    rounds, base = [], 0
+    while 2 ** len(rounds) < n_patch:
+        step = 2 ** len(rounds)
+        size = FF // (2 * step)
+        bit = lax.rem(patch // step, 2)
+        kept, sent = base + bit * size, base + (1 - bit) * size
+        rounds.append((patch + (1 - 2 * bit) * step, kept, sent, size))
+        base = kept
+    last_round = len(rounds) - 1
     loads = []
 
     def fetch(source, target):
@@ -76,7 +83,7 @@
         pl.semaphore_signal(
             barrier, inc=1, device_id={"view": lax.rem(view + d, n_view)}, device_id_type=MESH
         )
-    for _, to in patches:
+    for to, _, _, _ in rounds:
         pl.semaphore_signal(barrier, inc=1, device_id={"patch": to}, device_id_type=MESH)
 
     core_sum, core_share = 0, 1
@@ -101,15 +108,21 @@
     def sum_over_view(m, d):
         return remote(m, view_sum + d - 1, mid.at[m], view_in.at[m, d - 1], {"view": owner(m)[0]})
 
-    def sum_over_patch(m, d, to):
-        start = pl.multiple_of(to * piece, 16)
-        return remote(
-            m, patch_sum + d - 1, low.at[m, pl.ds(start, piece)], patch_in.at[m, d - 1], {"patch": to}
-        )
-
-    def share_over_patch(m, d, to):
-        own = full.at[m, pl.ds(pl.multiple_of(patch * piece, 16), piece)]
-        return remote(m, patch_share + d - 1, own, own, {"patch": to})
+    def rows(start, size):
+        return pl.ds(pl.multiple_of(start, 16), size)
+
+    def arrived(m, r):
+        size = rounds[r][3]
+        return patch_in.at[m, FF - 2 * size:FF - size]
+
+    def sum_over_patch(m, r):
+        to, _, sent, size = rounds[r]
+        return remote(m, patch_sum + r, low.at[m, rows(sent, size)], arrived(m, r), {"patch": to})
+
+    def share_over_patch(m, r):
+        to, kept, _, size = rounds[r]
+        own = full.at[m, rows(kept, size)]
+        return remote(m, patch_share + r, own, own, {"patch": to})
 
     def share_over_view(m, d):
         to = (owner(m)[0] + d) % n_view
@@ -163,20 +176,27 @@
                 sum_over_view(m, d).wait_recv()
                 total = total + view_in[m, d - 1].astype(fp)
             low[m] = total.astype(half_type)
-            for d, to in patches:
-                sum_over_patch(m, d, to).start()
-
-    def stage_gather(m):
-        @pl.when(at_owner(m))
-        def _():
-            own = pl.ds(pl.multiple_of(patch * piece, 16), piece)
-            total = low[m, own].astype(fp)
-            for d, to in patches:
-                sum_over_patch(m, d, to).wait_recv()
-                total = total + patch_in[m, d - 1].astype(fp)
-            full[m, own] = total.astype(half_type)
-            for d, to in patches:
-                share_over_patch(m, d, to).start()
+            sum_over_patch(m, 0).start()
+
+    def stage_halve(m, r):
+        @pl.when(at_owner(m))
+        def _():
+            _, kept, _, size = rounds[r]
+            own = rows(kept, size)
+            sum_over_patch(m, r).wait_recv()
+            total = (low[m, own].astype(fp) + arrived(m, r)[...].astype(fp)).astype(half_type)
+            if r < last_round:
+                low[m, own] = total
+                sum_over_patch(m, r + 1).start()
+            else:
+                full[m, own] = total
+                share_over_patch(m, r).start()
+
+    def stage_double(m, r):
+        @pl.when(at_owner(m))
+        def _():
+            share_over_patch(m, r).wait_recv()
+            share_over_patch(m, r - 1).start()
 
     def newton(x):
         gram = dot_tn(x, x).astype(half_type)
@@ -186,8 +206,7 @@
     def stage_update(m):
         @pl.when(at_owner(m))
         def _():
-            for d, to in patches:
-                share_over_patch(m, d, to).wait_recv()
+            share_over_patch(m, 0).wait_recv()
             summed = full[m].astype(fp)
             norm = jnp.sqrt(jnp.sum(summed * summed, keepdims=True)) + eps_small
             ortho = (summed * (1.0 / norm)).astype(half_type)
@@ -240,9 +259,9 @@
 
         @pl.when(at_owner(m))
         def _():
-            for d, to in patches:
-                sum_over_patch(m, d, to).wait_send()
-                share_over_patch(m, d, to).wait_send()
+            for r in range(len(rounds)):
+                sum_over_patch(m, r).wait_send()
+                share_over_patch(m, r).wait_send()
             for d in range(1, n_view):
                 share_over_view(m, d).wait_send()
 
@@ -268,7 +287,7 @@
 
     project(0)
     gradient(0)
-    pl.semaphore_wait(barrier, n_view + n_patch - 1)
+    pl.semaphore_wait(barrier, n_view + len(rounds))
     run(stage_core, first)
     project(1)
     run(stage_view, first)
@@ -286,15 +305,31 @@
             run(stage_view, last)
     get_out.wait()
     early, late, rest = range(0, 4), range(4, 8), range(8, MATS)
+    def halve(chosen, r):
+        for m in chosen:
+            stage_halve(m, r)
+
+    def double(chosen):
+        for r in range(last_round, 0, -1):
+            for m in chosen:
+                stage_double(m, r)
+
     run(stage_patch, early)
-    run(stage_gather, early)
+    for r in range(last_round + 1):
+        halve(early, r)
     run(stage_patch, late)
-    run(stage_gather, late)
+    double(early)
+    halve(late, 0)
+    run(stage_update, early)
+    for r in range(1, last_round + 1):
+        halve(late, r)
     run(stage_patch, rest)
-    run(stage_update, early)
-    run(stage_gather, rest)
+    double(late)
+    for r in range(last_round + 1):
+        halve(rest, r)
+    double(rest)
+    run(stage_spread, early)
     run(stage_update, late)
-    run(stage_spread, early)
     run(stage_update, rest)
     run(stage_spread, late)
     decode(0)
@@ -306,7 +341,6 @@
 
 def solution(mesh):
     n_view, n_patch = mesh.shape["view"], mesh.shape["patch"]
-    piece = FF // n_patch
     slots = 2 * (n_view + n_patch - 1)
 
     def local(tokens, w_kv, w_rate, fast_weights, queries, w_query, out_gain, w_out):
@@ -335,7 +369,7 @@
                 whole,
                 pltpu.VMEM((MATS, n_view - 1, FF, HD), half_type),
                 whole,
-                pltpu.VMEM((MATS, n_patch - 1, piece, HD), half_type),
+                whole,
                 whole,
                 whole,
                 pltpu.VMEM((asked, width), fp),

time: 61.3 us -> 66.9 us (1.091); the launches traced: 61.1 us -> 65.8 us
  Pallas kernels: 59.3 us -> 64.1 us
    pallas_call x1, Pallas kernels: 59.3 us -> 64.1 us  [local(): pl.pallas_call(functools.partial(kernel, n_view, n_patch), out_shape=jax....]
where the time goes in v4:
time: 66.9 us; the launch traced here: 65.8 us
  Pallas kernels  64.1 us (96%)
  local copies, waits for them, and re-layouts  1.77 us (3%)
    pallas_call x1, Pallas kernels, local(): pl.pallas_call(functools.partial(kernel, n_view, n_patch), out_shape=jax....  64.1 us
    unnamed x1, local copies, waits for them, and re-layouts  1.77 us

profile of v4, /device:TPU:7, one launch (start us, length us, event | category | flops | bytes accessed | tf_op | source)
XLA Modules:
  0.0 65.8 jit_solution(16235116172912517615)
XLA Ops:
  0.0 64.1 %shard_map.82 = bf16[256,768]{1,0:T(8,128)(2,1)} custom-call(bf16[256,768]{1,0:T(8,128)(2,1)} %tokens_hbm.1, bf16[768,1536]{1,0:T(8,128)(2,1)} %w_kv_hbm.1, bf16[3,768]{1,0:T(4,128)(2,1)} %w_rate.1, bf16[3,3,512,256]{3,2,1,0:T(8,128)(2,1)} %bitcast.1, bf16[256,768]{1,0:T(8,128)(2,1)} %queries_hbm.1, bf16[768,768]{1,0:T(8,128)(2,1)} %w_query_hbm.1, ...), custom_call_target="tpu_custom_call" | custom-call | tf_op jit(solution)/shard_map/pallas_call | solution.py:352
  64.1 1.8 %copy.10 = bf16[256,768]{1,0:T(8,128)(2,1)} copy(bf16[256,768]{1,0:T(8,128)(2,1)} %shard_map.82) | data formatting | bytes 786432
